TPU v7x, 32 devices: a whole 2x2x4 slice. The times are simulated.
32 devices in a mesh: groups: 2 (over x), img: 8 (over z, y), head: 2 (over core).
Axes of the slice: x: 2, y: 2, z: 4, core: 2. Of those that a mesh axis runs over, the one named last changes fastest.
Arguments:
- enc_tokens: bfloat16 [64, 32, 1024], P(('groups', 'img')), parts along dimension 0
- pairs: int32 [256, 2], P('groups'), parts along dimension 0, may hold values from 0 to 31, as said below
- live: int32 [16], P('groups'), parts along dimension 0, may hold values from 1 to 16, as said below
- proj_w: bfloat16 [1024, 768], replicated, may hold values from -0.1875 to 0.1875
- self_qkv: bfloat16 [768, 3, 768], P(None, None, 'head')
- self_out: bfloat16 [768, 768], P('head'), may hold values from -0.21875 to 0.21875
- cross_q: bfloat16 [768, 768], P(None, 'head')
- cross_kv: bfloat16 [768, 2, 768], P(None, None, 'head')
- cross_out: bfloat16 [768, 768], P('head'), may hold values from -0.21875 to 0.21875
- mlp_w1: bfloat16 [768, 3072], P(None, 'head'), may hold values from -0.21875 to 0.21875
- mlp_w2: bfloat16 [3072, 768], P('head'), may hold values from -0.109375 to 0.109375
- head_w: bfloat16 [768, 3712], P('img', 'head'), may hold values from -0.21875 to 0.21875
Outputs:
- joined_out: float32 [64, 3712, 32], P(('groups', 'img'), 'head'), parts along dimension 0
There are 2 independent parts, one for each index of `groups`. A program takes and returns all parts, laid end to end along the dimension named above; an argument that names none is the same for every part. Nothing has to cross between parts.
Inputs may be any that keep to these rules, and one draw needn't show every extreme that they name: `pairs`: rows o * 16 to o * 16 + 15 are the pair slots of owner o. The two images of a pair differ. Image i is held by img index i // 4. Among the 2 * live[o] pair sides of owner o's live slots, at most 4 name images held by one img index, and some owner reaches 4. `live`: some owner uses all 16 slots.
All inputs are finite; a program needn't handle non-finite values.
Results may differ from a plain program's by a relative error of at most 0.012.
Values may be sent and summed in bfloat16 or wider, within the bound.
A program may use at most 128 MiB of HBM per device.

v0:
```python
import functools

import jax
import jax.numpy as jnp
from jax import lax
from jax.experimental import pallas as pl
from jax.experimental.pallas import tpu as pltpu
from jax.sharding import PartitionSpec as P

HD = 64
EPS_NORM = 1e-06
F32 = jnp.float32
BF16 = jnp.bfloat16
MESH = pl.DeviceIdType.MESH


def normed(tensor):
    tensor = tensor.astype(F32)
    center = tensor - jnp.mean(tensor, axis=-1, keepdims=True)
    moment = jnp.mean(center * center, axis=-1, keepdims=True)
    return center * lax.rsqrt(moment + EPS_NORM)


def mm(a, b):
    return jnp.dot(a, b, preferred_element_type=F32)


def gelu(x):
    return 0.5 * x * (1.0 + lax.erf(x * (0.5**0.5)))


def attend(queries, key_rows, values, tok):
    rows, width = queries.shape
    row = lax.broadcasted_iota(jnp.int32, (rows, rows), 0) // tok
    col = lax.broadcasted_iota(jnp.int32, (rows, rows), 1) // tok
    same = row == col
    pair = 2 * HD
    first = lax.broadcasted_iota(jnp.int32, (1, pair), 1) < HD
    sides = (first.astype(F32).astype(BF16), 1 - first.astype(F32).astype(BF16))
    parts = []
    for at in range(0, width, pair):
        q2, k2, v2 = (x[:, at : at + pair] for x in (queries, key_rows, values))
        found = []
        for side in sides:
            scores = lax.dot_general(
                q2 * side, k2, (((1,), (1,)), ((), ())), preferred_element_type=F32
            )
            scores = jnp.where(same, scores * HD ** (-0.5), -jnp.inf)
            raised = jnp.exp(scores - jnp.max(scores, axis=-1, keepdims=True))
            probs = raised / jnp.sum(raised, axis=-1, keepdims=True)
            found.append(mm(probs.astype(BF16), v2))
        parts.append(jnp.where(first, found[0], found[1]).astype(BF16))
    return jnp.concatenate(parts, axis=1)


def kernel(
    n,
    ids_ref,
    sel_ref,
    enc_ref,
    proj_hbm,
    qkv_hbm,
    sout_hbm,
    cq_hbm,
    ckv_hbm,
    co_hbm,
    w1_hbm,
    w2_hbm,
    out_ref,
    proj,
    qkv,
    sout,
    cq,
    ckv,
    co,
    w1,
    w2,
    all_in,
    all_as,
    part_mine,
    part_theirs,
    asked,
    partner,
    fin,
    back_out,
    back_in,
    sums,
    load_sem,
    wsend_sem,
    wrecv_sem,
    gsend_sem,
    grecv_sem,
    fsend_sem,
    frecv_sem,
    bsend_sem,
    brecv_sem,
    xsend_sem,
    xrecv_sem,
):
    me = lax.axis_index("img")
    core = lax.axis_index("head")
    other = 1 - core
    img_dev, tok = all_in.shape[2], all_in.shape[3]
    rows = img_dev * tok
    width = out_ref.shape[1]
    half = width // 2
    count = asked.shape[0]
    sibling = {"head": other}

    def peer(step):
        return lax.rem(me + step, n)

    def remote(src, dst, send, recv, where):
        return pltpu.make_async_remote_copy(
            src_ref=src, dst_ref=dst, send_sem=send, recv_sem=recv, device_id=where,
            device_id_type=MESH,
        )

    hbm = (proj_hbm, qkv_hbm, sout_hbm, cq_hbm, ckv_hbm, co_hbm, w1_hbm, w2_hbm)
    dst = (proj, qkv, sout, cq.at[0], ckv.at[0], co.at[0], w1.at[0], w2.at[0])
    loads = [pltpu.make_async_copy(s, d, load_sem.at[i]) for i, (s, d) in enumerate(zip(hbm, dst))]
    for load in loads:
        load.start()

    barrier = pltpu.get_barrier_semaphore()
    pl.semaphore_signal(barrier, inc=1, device_id=sibling, device_id_type=MESH)

    @pl.loop(1, n)
    def _(step):
        pl.semaphore_signal(barrier, inc=1, device_id={"img": peer(step)}, device_id_type=MESH)

    pl.semaphore_wait(barrier, n)

    pieces = [
        remote(s, d.at[1], wsend_sem.at[i], wrecv_sem.at[i], sibling)
        for i, (s, d) in enumerate(
            ((cq_hbm, cq), (ckv_hbm, ckv), (co_hbm, co), (w1_hbm, w1), (w2_hbm, w2))
        )
    ]

    def spread(kind, ref):
        @pl.loop(1, n)
        def _(step):
            to = peer(step)
            remote(
                ref.at[me, core], ref.at[me, core], gsend_sem.at[kind, to],
                grecv_sem.at[kind, me], {"img": to},
            ).start()

    def forward(kind, ref):
        @pl.loop(1, n)
        def _(step):
            of = peer(step)
            block = ref.at[of, core]
            remote(
                block, block, gsend_sem.at[kind, of], grecv_sem.at[kind, of], {"img": of}
            ).wait_recv()
            remote(
                block, block, fsend_sem.at[kind, of], frecv_sem.at[kind, of], sibling
            ).start()

    def settle(kind, ref):
        @pl.loop(1, n)
        def _(step):
            of = peer(step)
            block = ref.at[of, other]
            remote(
                block, block, fsend_sem.at[kind, of], frecv_sem.at[kind, of], sibling
            ).wait_recv()

    def drain(kind, ref):
        @pl.loop(1, n)
        def _(step):
            of = peer(step)
            block = ref.at[me, core]
            remote(
                block, block, gsend_sem.at[kind, of], grecv_sem.at[kind, of], {"img": of}
            ).wait_send()
            block = ref.at[of, core]
            remote(
                block, block, fsend_sem.at[kind, of], frecv_sem.at[kind, of], sibling
            ).wait_send()

    def put(ref, value):
        for side in range(2):
            ref[me, side] = value[:, side * half : (side + 1) * half].reshape(img_dev, tok, half)

    loads[0].wait()
    tokens = mm(enc_ref[...], proj[...]).astype(BF16)
    self_in = normed(tokens).astype(BF16)
    put(all_in, self_in)
    spread(0, all_in)
    loads[1].wait()
    triple = mm(self_in, qkv[...]).astype(BF16)
    local = triple.shape[1] // 3
    context = attend(
        triple[:, :local], triple[:, local : 2 * local], triple[:, 2 * local :], tok
    )
    loads[2].wait()
    part_mine[...] = mm(context, sout[...])
    swap = remote(part_mine, part_theirs, xsend_sem.at[0], xrecv_sem.at[0], sibling)
    swap.start()
    for piece in pieces:
        piece.start()
    swap.wait()
    after_self = (tokens.astype(F32) + (part_mine[...] + part_theirs[...])).astype(BF16)
    put(all_as, after_self)
    spread(1, all_as)
    forward(0, all_in)
    forward(1, all_as)
    settle(0, all_in)
    settle(1, all_as)

    entries = count // tok

    @pl.loop(0, entries)
    def _(e):
        mine = ids_ref[core * entries + e]
        seen = ids_ref[core * entries + e + 1 - 2 * lax.rem(e, 2)]
        at = pl.ds(pl.multiple_of(e * tok, tok), tok)
        for side in range(2):
            lanes = slice(side * half, (side + 1) * half)
            asked[at, lanes] = all_as[mine // img_dev, side, lax.rem(mine, img_dev)]
            partner[at, lanes] = all_in[seen // img_dev, side, lax.rem(seen, img_dev)]

    for load in loads[3:]:
        load.wait()
    for piece in pieces:
        piece.wait()

    chunk = min(256, count)
    group = min(128, chunk)
    tile = 512

    @pl.loop(0, count // chunk)
    def _(step):
        at = pl.ds(pl.multiple_of(step * chunk, chunk), chunk)
        held = asked[at, :]
        query_in = normed(held).astype(BF16)
        seen_in = partner[at, :]

        def cross(side, total):
            asking = mm(query_in, cq[side]).astype(BF16)
            seen_kv = mm(seen_in, ckv[side]).astype(BF16)
            ctx = [
                attend(
                    asking[g : g + group], seen_kv[g : g + group, :local],
                    seen_kv[g : g + group, local:], tok,
                )
                for g in range(0, chunk, group)
            ]
            return total + mm(jnp.concatenate(ctx, axis=0), co[side])

        total = lax.fori_loop(0, 2, cross, held.astype(F32))
        after_cross = total.astype(BF16)
        mlp_in = normed(after_cross).astype(BF16)
        total = after_cross.astype(F32)
        for tile_at in range(0, w1.shape[2], tile):
            def hidden(side, total, tile_at=tile_at):
                up = gelu(mm(mlp_in, w1[side, :, tile_at : tile_at + tile])).astype(BF16)
                return total + mm(up, w2[side, tile_at : tile_at + tile, :])

            total = lax.fori_loop(0, 2, hidden, total)
        final_in = normed(total.astype(BF16)).astype(BF16)
        for side in range(2):
            fin[core, side, at, :] = final_in[:, side * half : (side + 1) * half]

    trade = remote(
        fin.at[core, other], fin.at[core, other], xsend_sem.at[1], xrecv_sem.at[1], sibling
    )
    trade.start()
    trade.wait_recv()

    row = lax.broadcasted_iota(jnp.int32, (rows, count), 0)
    col = lax.broadcasted_iota(jnp.int32, (rows, count), 1)
    aligned = lax.rem(row, tok) == lax.rem(col, tok)

    def gathered(owner):
        image = owner * img_dev + row // tok
        total = None
        for part in range(2):
            chosen = aligned & (sel_ref[:, part * count : (part + 1) * count] == image)
            term = mm(jnp.where(chosen, 1.0, 0.0).astype(BF16), fin[part, core])
            total = term if total is None else total + term
        return total

    @pl.loop(1, n)
    def _(step):
        to = peer(step)
        back_out[to] = gathered(to).astype(BF16)
        remote(
            back_out.at[to], back_in.at[me], bsend_sem.at[to], brecv_sem.at[me], {"img": to}
        ).start()

    sums[core] = gathered(me)

    @pl.loop(1, n)
    def _(step):
        of = peer(step)
        remote(
            back_out.at[of], back_in.at[of], bsend_sem.at[of], brecv_sem.at[of], {"img": of}
        ).wait_recv()
        sums[core] += back_in[of].astype(F32)

    last = remote(sums.at[core], sums.at[core], xsend_sem.at[2], xrecv_sem.at[2], sibling)
    last.start()
    last.wait()
    out_ref[:, :half] = sums[0]
    out_ref[:, half:] = sums[1]

    trade.wait_send()
    drain(0, all_in)
    drain(1, all_as)

    @pl.loop(1, n)
    def _(step):
        of = peer(step)
        remote(
            back_out.at[of], back_in.at[of], bsend_sem.at[of], brecv_sem.at[of], {"img": of}
        ).wait_send()


def on_device(
    enc_tokens,
    pairs,
    live,
    proj_w,
    self_qkv,
    self_out,
    cross_q,
    cross_kv,
    cross_out,
    mlp_w1,
    mlp_w2,
    head_w,
):
    n = lax.axis_size("img")
    me = lax.axis_index("img")
    img_dev, tok, enc_width = enc_tokens.shape
    rows = img_dev * tok
    width, local = cross_q.shape
    half = width // 2
    entry_total = 2 * pairs.shape[0] // n
    table = pairs.reshape(n, entry_total)
    active = jnp.arange(entry_total)[None, :] // 2 < live[:, None]
    my_images = me * img_dev + jnp.arange(img_dev)
    named = (table[:, :, None] == my_images[None, None, :]) & active[:, :, None]
    counts = jnp.sum(named.astype(F32), axis=(0, 1))
    ids = lax.dynamic_index_in_dim(table, me, 0, keepdims=False)
    on = lax.dynamic_index_in_dim(active, me, 0, keepdims=False)
    sel = jnp.repeat(jnp.where(on, ids, -1), tok)[None, :]
    head_full = lax.all_gather(head_w, "img", axis=0, tiled=True)

    count = entry_total * tok // 2
    hidden = mlp_w1.shape[1]
    vmem = pl.BlockSpec(memory_space=pltpu.VMEM)
    sem = pltpu.SemaphoreType.DMA
    anywhere = pl.BlockSpec(memory_space=pl.ANY)
    totals = pl.pallas_call(
        functools.partial(kernel, n),
        out_shape=jax.ShapeDtypeStruct((rows, width), F32),
        in_specs=[pl.BlockSpec(memory_space=pltpu.SMEM), vmem, vmem] + [anywhere] * 8,
        out_specs=vmem,
        scratch_shapes=[
            pltpu.VMEM(proj_w.shape, BF16),
            pltpu.VMEM((width, 3 * local), BF16),
            pltpu.VMEM(self_out.shape, BF16),
            pltpu.VMEM((2, width, local), BF16),
            pltpu.VMEM((2, width, 2 * local), BF16),
            pltpu.VMEM((2, local, width), BF16),
            pltpu.VMEM((2, width, hidden), BF16),
            pltpu.VMEM((2, hidden, width), BF16),
            pltpu.VMEM((n, 2, img_dev, tok, half), BF16),
            pltpu.VMEM((n, 2, img_dev, tok, half), BF16),
            pltpu.VMEM((rows, width), F32),
            pltpu.VMEM((rows, width), F32),
            pltpu.VMEM((count, width), BF16),
            pltpu.VMEM((count, width), BF16),
            pltpu.VMEM((2, 2, count, half), BF16),
            pltpu.VMEM((n, rows, half), BF16),
            pltpu.VMEM((n, rows, half), BF16),
            pltpu.VMEM((2, rows, half), F32),
            sem((8,)),
            sem((5,)),
            sem((5,)),
            sem((2, n)),
            sem((2, n)),
            sem((2, n)),
            sem((2, n)),
            sem((n,)),
            sem((n,)),
            sem((3,)),
            sem((3,)),
        ],
        compiler_params=pltpu.CompilerParams(
            collective_id=0, has_side_effects=True, vmem_limit_bytes=56 * 1024 * 1024
        ),
        cost_estimate=pl.CostEstimate(
            flops=12_000_000_000, bytes_accessed=20_000_000, transcendentals=2_000_000
        ),
    )(
        ids,
        sel,
        enc_tokens.reshape(rows, enc_width),
        proj_w,
        self_qkv.reshape(width, 3 * local),
        self_out,
        cross_q,
        cross_kv.reshape(width, 2 * local),
        cross_out,
        mlp_w1,
        mlp_w2,
    )
    totals = totals.reshape(img_dev, tok, width)
    coarse = lax.reduce_precision(totals, 8, 7)
    both = jnp.concatenate([coarse, totals - coarse], axis=1).astype(BF16)
    out = jnp.einsum("ind,dc->inc", both, head_full, preferred_element_type=F32)
    out = (out[:, :tok] + out[:, tok:]) / jnp.maximum(counts, 1.0)[:, None, None]
    return jnp.transpose(out, (0, 2, 1))


def solution(mesh):
    placed = (
        P(("groups", "img"), None, None),
        P("groups", None),
        P("groups"),
        P(),
        P(None, None, "head"),
        P("head", None),
        P(None, "head"),
        P(None, None, "head"),
        P("head", None),
        P(None, "head"),
        P("head", None),
        P("img", "head"),
    )
    return jax.shard_map(
        on_device,
        mesh=mesh,
        in_specs=placed,
        out_specs=P(("groups", "img"), "head", None),
        check_vma=False,
    )
```

profile of v0, /device:TPU:23, one launch (start us, length us, event | category | flops | bytes accessed | tf_op | source)
XLA Modules:
  0.0 140.4 jit_solution(15514455666741322866)
XLA Ops:
  6.5 0.0 all-gather.2.cloned.1.call-start
  6.5 0.7 all-gather.2.cloned.1.call-update
  7.3 0.8 copy.17
  8.0 0.1 reshape.87
  8.1 0.7 broadcast_compare_fusion
  8.9 0.1 broadcast_in_dim.3
  9.0 0.7 broadcast_in_dim_reshape.4.sel_ref
  9.6 2.6 %copy.18 = bf16[768,3,384]{0,2,1:T(8,128)(2,1)S(1)} copy(bf16[768,3,384]{2,0,1:T(8,128)(2,1)} %param.16) | data formatting | bytes 3538944 | tf_op args[4]
  12.3 0.0 copy-start
  12.3 2.2 %copy.19.qkv_hbm = bf16[768,1152]{1,0:T(8,128)(2,1)} copy(bf16[768,1152]{0,1:T(8,128)(2,1)S(1)} %bitcast.16) | data formatting | bytes 3538944 | tf_op jit(solution)/shard_map/reshape | solution.py:406
  14.5 0.0 copy-done
  14.5 1.3 copy.20
  15.8 0.5 dynamic-slice_bitcast_fusion.ids_ref
  16.3 0.2 convert_reduce_fusion
  16.5 112.1 %shard_map.118 = f32[128,768]{1,0:T(8,128)} custom-call(s32[32]{0:T(128)} %dynamic-slice_bitcast_fusion.ids_ref, s32[1,1024]{1,0:T(1,128)} %broadcast_in_dim_reshape.4.sel_ref, bf16[128,1024]{1,0:T(8,128)(2,1)} %bitcast.20, bf16[1024,768]{1,0:T(8,128)(2,1)} %proj_hbm.1, bf16[768,1152]{1,0:T(8,128)(2,1)} %copy.19.qkv_hbm, bf16[384,768]{1,0:T(8,128)(2,1)} %sout_hbm.1, ...), custom_call_target="tpu_custom_call" | custom-call | flops 12000000000 | bytes 20000000 | tf_op jit(solution)/shard_map/pallas_call | solution.py:359
  128.6 1.0 reduce-precision_convert_fusion
  129.6 0.0 all-gather.2.cloned.1.call-done
  129.7 2.8 %fusion = f32[4,64,1856]{2,1,0:T(8,128)S(1)} fusion(bf16[768,1856]{1,0:T(8,128)(2,1)} %all-gather.2.cloned.1.call-done, bf16[4,32,768]{2,1,0:T(8,128)(2,1)S(1)} %get-tuple-element.6, bf16[4,32,768]{2,1,0:T(8,128)(2,1)S(1)} %get-tuple-element.5), kind=kOutput, calls=%fused_computation | convolution fusion | flops 730595328 | bytes 5144576 | tf_op jit(solution)/shard_map/ind,dc->inc/dot_general | solution.py:417
  132.5 1.1 fusion.3
  (4 shorter events, 0.0 us)
Async XLA Ops:
  6.5 123.1 %all-gather.2.cloned.1.call-start = ((), (), s32[]{:S(2)}) async-start(), calls=%async_computation | async-start | bytes 3317760 | tf_op jit(solution)/shard_map/all_gather | solution.py:352
  12.3 2.2 %copy-start = (bf16[768,2,384]{2,1,0:T(2,128)(2,1)S(1)}, bf16[768,2,384]{2,1,0:T(2,128)(2,1)}, u32[]{:S(2)}) copy-start(bf16[768,2,384]{2,1,0:T(2,128)(2,1)} %param.19) | copy-start | bytes 3538948
Sparse Core Ops, SparseCore 0:
  9.5 80.6 all-gather.1
where the time goes:
time: 141 us; the launch traced here: 140 us
  Pallas kernels  112 us (79%)
  between operations  13.4 us (10%)
  local copies, waits for them, and re-layouts  8.3 us (6%)
  other arithmetic  3.07 us (2%)
  matrix products  2.81 us (2%)
    pallas_call x1, Pallas kernels, on_device(): pl.pallas_call(functools.partial(kernel, n), out_shape=jax.ShapeDtypeStru...  112 us
    unnamed x5, local copies, waits for them, and re-layouts  4.7 us
  transfers between devices with their start and end apart: 1, of which 0 were waited for; matrix products, arithmetic and copies ran while one was open for 7% of the time, Pallas kernels for 80%

commit v1 on v0

--- a/solution.py
+++ b/solution.py
@@ -66,7 +66,9 @@
     co_hbm,
     w1_hbm,
     w2_hbm,
+    head_hbm,
     out_ref,
+    head_ref,
     proj,
     qkv,
     sout,
@@ -83,16 +85,20 @@
     partner,
     fin,
     back_out,
+    across,
     back_in,
     sums,
     load_sem,
+    hload_sem,
     wsend_sem,
     wrecv_sem,
     gsend_sem,
     grecv_sem,
+    ysend_sem,
     fsend_sem,
     frecv_sem,
     bsend_sem,
+    arecv_sem,
     brecv_sem,
     xsend_sem,
     xrecv_sem,
@@ -107,8 +113,12 @@
     count = asked.shape[0]
     sibling = {"head": other}
 
+    lines = n // 2
+    line, lane = me // 2, lax.rem(me, 2)
+    mate = me + 1 - 2 * lane
+
     def peer(step):
-        return lax.rem(me + step, n)
+        return lax.rem(line + step, lines) * 2 + lane
 
     def remote(src, dst, send, recv, where):
         return pltpu.make_async_remote_copy(
@@ -125,11 +135,13 @@
     barrier = pltpu.get_barrier_semaphore()
     pl.semaphore_signal(barrier, inc=1, device_id=sibling, device_id_type=MESH)
 
-    @pl.loop(1, n)
+    pl.semaphore_signal(barrier, inc=1, device_id={"img": mate}, device_id_type=MESH)
+
+    @pl.loop(1, lines)
     def _(step):
         pl.semaphore_signal(barrier, inc=1, device_id={"img": peer(step)}, device_id_type=MESH)
 
-    pl.semaphore_wait(barrier, n)
+    pl.semaphore_wait(barrier, lines + 1)
 
     pieces = [
         remote(s, d.at[1], wsend_sem.at[i], wrecv_sem.at[i], sibling)
@@ -138,48 +150,83 @@
         )
     ]
 
-    def spread(kind, ref):
-        @pl.loop(1, n)
+    def spread(kind, src, view):
+        @pl.loop(1, lines)
         def _(step):
             to = peer(step)
             remote(
-                ref.at[me, core], ref.at[me, core], gsend_sem.at[kind, to],
-                grecv_sem.at[kind, me], {"img": to},
+                src, view(me), gsend_sem.at[kind, to], grecv_sem.at[kind, me], {"img": to}
             ).start()
 
-    def forward(kind, ref):
+        remote(
+            src, view(me), gsend_sem.at[kind, mate], grecv_sem.at[kind, me], {"img": mate}
+        ).start()
+
+    def arrival(kind, view, of):
+        remote(
+            view(of), view(of), gsend_sem.at[kind, of], grecv_sem.at[kind, of], {"img": mate}
+        ).wait_recv()
+
+    def crossing(kind, view, of):
+        return remote(
+            view(of), view(of), ysend_sem.at[kind, of], grecv_sem.at[kind, of], {"img": mate}
+        )
+
+    def handing(kind, view, of):
+        return remote(
+            view(of), view(of), fsend_sem.at[kind, of], frecv_sem.at[kind, of], sibling
+        )
+
+    def forward(kind, view, hand=True):
+        @pl.loop(1, lines)
+        def _(step):
+            of = peer(step)
+            arrival(kind, view, of)
+            crossing(kind, view, of).start()
+            if hand:
+                handing(kind, view, of).start()
+
+    def settle(kind, view, hand=True):
+        @pl.loop(0, lines)
+        def _(step):
+            of = peer(step) + 1 - 2 * lane
+            arrival(kind, view, of)
+            if hand:
+                handing(kind, view, of).start()
+
+    def receive(kind, view):
         @pl.loop(1, n)
         def _(step):
-            of = peer(step)
-            block = ref.at[of, core]
+            handing(kind, view, lax.rem(me + step, n)).wait_recv()
+
+    def drain(kind, view, hand=True):
+        @pl.loop(1, lines)
+        def _(step):
+            to = peer(step)
             remote(
-                block, block, gsend_sem.at[kind, of], grecv_sem.at[kind, of], {"img": of}
-            ).wait_recv()
-            remote(
-                block, block, fsend_sem.at[kind, of], frecv_sem.at[kind, of], sibling
-            ).start()
-
-    def settle(kind, ref):
-        @pl.loop(1, n)
-        def _(step):
-            of = peer(step)
-            block = ref.at[of, other]
-            remote(
-                block, block, fsend_sem.at[kind, of], frecv_sem.at[kind, of], sibling
-            ).wait_recv()
-
-    def drain(kind, ref):
-        @pl.loop(1, n)
-        def _(step):
-            of = peer(step)
-            block = ref.at[me, core]
-            remote(
-                block, block, gsend_sem.at[kind, of], grecv_sem.at[kind, of], {"img": of}
+                view(me), view(me), gsend_sem.at[kind, to], grecv_sem.at[kind, me], {"img": to}
             ).wait_send()
-            block = ref.at[of, core]
-            remote(
-                block, block, fsend_sem.at[kind, of], frecv_sem.at[kind, of], sibling
-            ).wait_send()
+            crossing(kind, view, to).wait_send()
+
+        remote(
+            view(me), view(me), gsend_sem.at[kind, mate], grecv_sem.at[kind, me], {"img": mate}
+        ).wait_send()
+        if hand:
+            @pl.loop(1, n)
+            def _(step):
+                handing(kind, view, lax.rem(me + step, n)).wait_send()
+
+    def in_view(side):
+        return lambda of: all_in.at[of, side]
+
+    def as_view(side):
+        return lambda of: all_as.at[of, side]
+
+    def head_view(of):
+        return head_ref.at[of]
+
+    own_head = pltpu.make_async_copy(head_hbm, head_ref.at[me], hload_sem.at[0])
+    own_head.start()
 
     def put(ref, value):
         for side in range(2):
@@ -189,7 +236,7 @@
     tokens = mm(enc_ref[...], proj[...]).astype(BF16)
     self_in = normed(tokens).astype(BF16)
     put(all_in, self_in)
-    spread(0, all_in)
+    spread(0, all_in.at[me, core], in_view(core))
     loads[1].wait()
     triple = mm(self_in, qkv[...]).astype(BF16)
     local = triple.shape[1] // 3
@@ -205,11 +252,14 @@
     swap.wait()
     after_self = (tokens.astype(F32) + (part_mine[...] + part_theirs[...])).astype(BF16)
     put(all_as, after_self)
-    spread(1, all_as)
-    forward(0, all_in)
-    forward(1, all_as)
-    settle(0, all_in)
-    settle(1, all_as)
+    spread(1, all_as.at[me, core], as_view(core))
+    forward(0, in_view(core))
+    forward(1, as_view(core))
+    settle(0, in_view(core))
+    settle(1, as_view(core))
+    spread(2, head_hbm, head_view)
+    receive(0, in_view(other))
+    receive(1, as_view(other))
 
     entries = count // tok
 
@@ -234,6 +284,10 @@
 
     @pl.loop(0, count // chunk)
     def _(step):
+        @pl.when(step == count // chunk - 1)
+        def _():
+            forward(2, head_view, hand=False)
+
         at = pl.ds(pl.multiple_of(step * chunk, chunk), chunk)
         held = asked[at, :]
         query_in = normed(held).astype(BF16)
@@ -284,23 +338,44 @@
             total = term if total is None else total + term
         return total
 
-    @pl.loop(1, n)
+    def over(block):
+        return remote(
+            back_out.at[block], across.at[block // 2], bsend_sem.at[block],
+            arecv_sem.at[block // 2], {"img": mate},
+        )
+
+    def along(to):
+        return remote(
+            back_out.at[to], back_in.at[line], bsend_sem.at[to], brecv_sem.at[line], {"img": to}
+        )
+
+    @pl.loop(0, lines)
+    def _(step):
+        block = peer(step + 1) + 1 - 2 * lane
+        back_out[block] = gathered(block).astype(BF16)
+        over(block).start()
+
+    def joined(block):
+        total = gathered(block)
+        over(block).wait_recv()
+        return total + across[block // 2].astype(F32)
+
+    @pl.loop(1, lines)
     def _(step):
         to = peer(step)
-        back_out[to] = gathered(to).astype(BF16)
-        remote(
-            back_out.at[to], back_in.at[me], bsend_sem.at[to], brecv_sem.at[me], {"img": to}
-        ).start()
-
-    sums[core] = gathered(me)
-
-    @pl.loop(1, n)
+        back_out[to] = joined(to).astype(BF16)
+        along(to).start()
+
+    sums[core] = joined(me)
+
+    @pl.loop(1, lines)
     def _(step):
         of = peer(step)
         remote(
-            back_out.at[of], back_in.at[of], bsend_sem.at[of], brecv_sem.at[of], {"img": of}
+            back_out.at[of], back_in.at[of // 2], bsend_sem.at[of], brecv_sem.at[of // 2],
+            {"img": of},
         ).wait_recv()
-        sums[core] += back_in[of].astype(F32)
+        sums[core] += back_in[of // 2].astype(F32)
 
     last = remote(sums.at[core], sums.at[core], xsend_sem.at[2], xrecv_sem.at[2], sibling)
     last.start()
@@ -309,15 +384,19 @@
     out_ref[:, half:] = sums[1]
 
     trade.wait_send()
-    drain(0, all_in)
-    drain(1, all_as)
-
-    @pl.loop(1, n)
-    def _(step):
-        of = peer(step)
-        remote(
-            back_out.at[of], back_in.at[of], bsend_sem.at[of], brecv_sem.at[of], {"img": of}
-        ).wait_send()
+    settle(2, head_view, hand=False)
+    own_head.wait()
+    drain(0, in_view(core))
+    drain(1, as_view(core))
+    drain(2, head_view, hand=False)
+
+    @pl.loop(0, lines)
+    def _(step):
+        over(peer(step) + 1 - 2 * lane).wait_send()
+
+    @pl.loop(1, lines)
+    def _(step):
+        along(peer(step)).wait_send()
 
 
 def on_device(
@@ -349,18 +428,20 @@
     ids = lax.dynamic_index_in_dim(table, me, 0, keepdims=False)
     on = lax.dynamic_index_in_dim(active, me, 0, keepdims=False)
     sel = jnp.repeat(jnp.where(on, ids, -1), tok)[None, :]
-    head_full = lax.all_gather(head_w, "img", axis=0, tiled=True)
 
     count = entry_total * tok // 2
     hidden = mlp_w1.shape[1]
     vmem = pl.BlockSpec(memory_space=pltpu.VMEM)
     sem = pltpu.SemaphoreType.DMA
     anywhere = pl.BlockSpec(memory_space=pl.ANY)
-    totals = pl.pallas_call(
+    totals, head_all = pl.pallas_call(
         functools.partial(kernel, n),
-        out_shape=jax.ShapeDtypeStruct((rows, width), F32),
-        in_specs=[pl.BlockSpec(memory_space=pltpu.SMEM), vmem, vmem] + [anywhere] * 8,
-        out_specs=vmem,
+        out_shape=(
+            jax.ShapeDtypeStruct((rows, width), F32),
+            jax.ShapeDtypeStruct((n, *head_w.shape), BF16),
+        ),
+        in_specs=[pl.BlockSpec(memory_space=pltpu.SMEM), vmem, vmem] + [anywhere] * 9,
+        out_specs=(vmem, anywhere),
         scratch_shapes=[
             pltpu.VMEM(proj_w.shape, BF16),
             pltpu.VMEM((width, 3 * local), BF16),
@@ -378,17 +459,21 @@
             pltpu.VMEM((count, width), BF16),
             pltpu.VMEM((2, 2, count, half), BF16),
             pltpu.VMEM((n, rows, half), BF16),
-            pltpu.VMEM((n, rows, half), BF16),
+            pltpu.VMEM((n // 2, rows, half), BF16),
+            pltpu.VMEM((n // 2, rows, half), BF16),
             pltpu.VMEM((2, rows, half), F32),
             sem((8,)),
+            sem((1,)),
             sem((5,)),
             sem((5,)),
-            sem((2, n)),
-            sem((2, n)),
+            sem((3, n)),
+            sem((3, n)),
+            sem((3, n)),
             sem((2, n)),
             sem((2, n)),
             sem((n,)),
-            sem((n,)),
+            sem((n // 2,)),
+            sem((n // 2,)),
             sem((3,)),
             sem((3,)),
         ],
@@ -410,7 +495,9 @@
         cross_out,
         mlp_w1,
         mlp_w2,
+        head_w,
     )
+    head_full = head_all.reshape(width, head_w.shape[1])
     totals = totals.reshape(img_dev, tok, width)
     coarse = lax.reduce_precision(totals, 8, 7)
     both = jnp.concatenate([coarse, totals - coarse], axis=1).astype(BF16)

time: 141 us -> 113 us (0.80)
  the two profiles are of different devices: /device:TPU:23 before, /device:TPU:0 now
where the time goes in v1:
time: 113 us; the launch traced here: 112 us
  Pallas kernels  98.5 us (87%)
  local copies, waits for them, and re-layouts  7.86 us (7%)
  other arithmetic  3.19 us (3%)
  matrix products  2.83 us (3%)
    pallas_call x1, Pallas kernels, on_device(): pl.pallas_call(functools.partial(kernel, n), out_shape=(jax.ShapeDtypeStr...  98.5 us
    unnamed x5, local copies, waits for them, and re-layouts  4.28 us
    dot_general x1, matrix products, on_device(): out = jnp.einsum('ind,dc->inc', both, head_full, preferred_element_type=F32)  2.83 us

profile of v1, /device:TPU:0, one launch (start us, length us, event | category | flops | bytes accessed | tf_op | source)
XLA Modules:
  0.0 112.4 jit_solution(6202980622111666261)
XLA Ops:
  0.0 0.0 copy-start
  0.0 0.9 broadcast_compare_fusion
  0.9 0.8 copy.19
  1.7 0.1 reshape.90
  1.7 0.2 convert_reduce_fusion
  1.9 0.5 dynamic-slice_bitcast_fusion.ids_ref
  2.5 0.1 broadcast_in_dim.3
  2.5 0.7 broadcast_in_dim_reshape.4.sel_ref
  3.2 2.5 %copy.25 = bf16[96,8,2,384]{3,1,2,0:T(8,128)(2,1)} copy(bf16[96,8,2,384]{3,2,1,0:T(2,128)(2,1)} %bitcast.18) | data formatting | bytes 2359296
  5.8 0.0 copy-done
  5.8 0.9 copy.20
  6.7 2.2 %copy.21.qkv_hbm = bf16[768,1152]{1,0:T(8,128)(2,1)} copy(bf16[768,1152]{0,1:T(8,128)(2,1)S(1)} %bitcast.17) | data formatting | bytes 3538944 | tf_op jit(solution)/shard_map/reshape | solution.py:491
  8.9 98.5 %shard_map.118 = (f32[128,768]{1,0:T(8,128)}, bf16[8,96,1856]{2,1,0:T(8,128)(2,1)}) custom-call(s32[32]{0:T(128)} %dynamic-slice_bitcast_fusion.ids_ref, s32[1,1024]{1,0:T(1,128)} %broadcast_in_dim_reshape.4.sel_ref, bf16[128,1024]{1,0:T(8,128)(2,1)} %bitcast.21, bf16[1024,768]{1,0:T(8,128)(2,1)} %proj_hbm.1, bf16[768,1152]{1,0:T(8,128)(2,1)} %copy.21.qkv_hbm, ...), custom_call_target="tpu_custom_call" | custom-call | flops 12000000000 | bytes 20000000 | tf_op jit(solution)/shard_map/pallas_call | solution.py:437
  107.4 1.0 reduce-precision_convert_fusion
  108.5 2.8 %fusion.3 = f32[4,64,1856]{2,1,0:T(8,128)S(1)} fusion(bf16[768,1856,1]{1,0,2:T(8,128)(2,1)} %bitcast.22, bf16[4,32,768]{2,1,0:T(8,128)(2,1)S(1)} %get-tuple-element.10, bf16[4,32,768]{2,1,0:T(8,128)(2,1)S(1)} %get-tuple-element.9), kind=kOutput, calls=%fused_computation.6 | convolution fusion | flops 730595328 | bytes 5144576 | tf_op jit(solution)/shard_map/ind,dc->inc/dot_general | solution.py:504
  111.3 1.1 fusion.1
  (4 shorter events, 0.0 us)
Async XLA Ops:
  0.0 5.8 %copy-start = (bf16[768,3,384]{2,0,1:T(8,128)(2,1)S(1)}, bf16[768,3,384]{2,0,1:T(8,128)(2,1)}, u32[]{:S(2)}) copy-start(bf16[768,3,384]{2,0,1:T(8,128)(2,1)} %param.16) | copy-start | bytes 5308420

commit v2 on v1

--- a/solution.py
+++ b/solution.py
@@ -36,7 +36,8 @@
     same = row == col
     pair = 2 * HD
     first = lax.broadcasted_iota(jnp.int32, (1, pair), 1) < HD
-    sides = (first.astype(F32).astype(BF16), 1 - first.astype(F32).astype(BF16))
+    scale = HD ** (-0.5)
+    sides = [jnp.where(on, scale, 0.0).astype(BF16) for on in (first, ~first)]
     parts = []
     for at in range(0, width, pair):
         q2, k2, v2 = (x[:, at : at + pair] for x in (queries, key_rows, values))
@@ -45,9 +46,9 @@
             scores = lax.dot_general(
                 q2 * side, k2, (((1,), (1,)), ((), ())), preferred_element_type=F32
             )
-            scores = jnp.where(same, scores * HD ** (-0.5), -jnp.inf)
+            scores = jnp.where(same, scores, -jnp.inf)
             raised = jnp.exp(scores - jnp.max(scores, axis=-1, keepdims=True))
-            probs = raised / jnp.sum(raised, axis=-1, keepdims=True)
+            probs = raised * (1.0 / jnp.sum(raised, axis=-1, keepdims=True))
             found.append(mm(probs.astype(BF16), v2))
         parts.append(jnp.where(first, found[0], found[1]).astype(BF16))
     return jnp.concatenate(parts, axis=1)
@@ -108,7 +109,7 @@
     other = 1 - core
     img_dev, tok = all_in.shape[2], all_in.shape[3]
     rows = img_dev * tok
-    width = out_ref.shape[1]
+    width = out_ref.shape[2]
     half = width // 2
     count = asked.shape[0]
     sibling = {"head": other}
@@ -380,8 +381,13 @@
     last = remote(sums.at[core], sums.at[core], xsend_sem.at[2], xrecv_sem.at[2], sibling)
     last.start()
     last.wait()
-    out_ref[:, :half] = sums[0]
-    out_ref[:, half:] = sums[1]
+    for side in range(2):
+        lanes = slice(side * half, (side + 1) * half)
+        whole = sums[side]
+        coarse = whole.astype(BF16)
+        rest = (whole - coarse.astype(F32)).astype(BF16)
+        out_ref[:, :tok, lanes] = coarse.reshape(img_dev, tok, half)
+        out_ref[:, tok:, lanes] = rest.reshape(img_dev, tok, half)
 
     trade.wait_send()
     settle(2, head_view, hand=False)
@@ -434,10 +440,10 @@
     vmem = pl.BlockSpec(memory_space=pltpu.VMEM)
     sem = pltpu.SemaphoreType.DMA
     anywhere = pl.BlockSpec(memory_space=pl.ANY)
-    totals, head_all = pl.pallas_call(
+    both, head_all = pl.pallas_call(
         functools.partial(kernel, n),
         out_shape=(
-            jax.ShapeDtypeStruct((rows, width), F32),
+            jax.ShapeDtypeStruct((img_dev, 2 * tok, width), BF16),
             jax.ShapeDtypeStruct((n, *head_w.shape), BF16),
         ),
         in_specs=[pl.BlockSpec(memory_space=pltpu.SMEM), vmem, vmem] + [anywhere] * 9,
@@ -498,9 +504,6 @@
         head_w,
     )
     head_full = head_all.reshape(width, head_w.shape[1])
-    totals = totals.reshape(img_dev, tok, width)
-    coarse = lax.reduce_precision(totals, 8, 7)
-    both = jnp.concatenate([coarse, totals - coarse], axis=1).astype(BF16)
     out = jnp.einsum("ind,dc->inc", both, head_full, preferred_element_type=F32)
     out = (out[:, :tok] + out[:, tok:]) / jnp.maximum(counts, 1.0)[:, None, None]
     return jnp.transpose(out, (0, 2, 1))

time: 113 us -> 112 us (level)
  no operation moved by 1% of the time
where the time goes in v2:
time: 112 us; the launch traced here: 111 us
  Pallas kernels  98.5 us (88%)
  local copies, waits for them, and re-layouts  7.85 us (7%)
  matrix products  2.95 us (3%)
  other arithmetic  2.14 us (2%)
    pallas_call x1, Pallas kernels, on_device(): pl.pallas_call(functools.partial(kernel, n), out_shape=(jax.ShapeDtypeStr...  98.5 us
    unnamed x5, local copies, waits for them, and re-layouts  4.28 us
    dot_general x1, matrix products, on_device(): out = jnp.einsum('ind,dc->inc', both, head_full, preferred_element_type=F32)  2.95 us

profile of v2, /device:TPU:0, one launch (start us, length us, event | category | flops | bytes accessed | tf_op | source)
XLA Modules:
  0.0 111.5 jit_solution(10304635689555418953)
XLA Ops:
  0.0 0.0 copy-start
  0.0 0.9 broadcast_compare_fusion
  0.9 0.8 copy.19
  1.7 0.1 reshape.87
  1.7 0.2 convert_reduce_fusion
  1.9 0.5 dynamic-slice_bitcast_fusion.ids_ref
  2.5 0.1 broadcast_in_dim.3
  2.5 0.7 broadcast_in_dim_reshape.4.sel_ref
  3.2 2.6 %copy.25 = bf16[96,8,2,384]{3,1,2,0:T(8,128)(2,1)} copy(bf16[96,8,2,384]{3,2,1,0:T(2,128)(2,1)} %bitcast.19) | data formatting | bytes 2359296
  5.8 0.0 copy-done
  5.8 0.9 copy.20
  6.7 2.2 %copy.21.qkv_hbm = bf16[768,1152]{1,0:T(8,128)(2,1)} copy(bf16[768,1152]{0,1:T(8,128)(2,1)S(1)} %bitcast.17) | data formatting | bytes 3538944 | tf_op jit(solution)/shard_map/reshape | solution.py:497
  8.9 98.5 %shard_map.118 = (bf16[4,64,768]{2,1,0:T(8,128)(2,1)}, bf16[8,96,1856]{2,1,0:T(8,128)(2,1)}) custom-call(s32[32]{0:T(128)} %dynamic-slice_bitcast_fusion.ids_ref, s32[1,1024]{1,0:T(1,128)} %broadcast_in_dim_reshape.4.sel_ref, bf16[128,1024]{1,0:T(8,128)(2,1)} %bitcast.21, bf16[1024,768]{1,0:T(8,128)(2,1)} %proj_hbm.1, bf16[768,1152]{1,0:T(8,128)(2,1)} %copy.21.qkv_hbm, ...), custom_call_target="tpu_custom_call" | custom-call | flops 12000000000 | bytes 20000000 | tf_op jit(solution)/shard_map/pallas_call | solution.py:443
  107.4 2.9 %fusion.2 = f32[4,64,1856]{2,1,0:T(8,128)S(1)} fusion(bf16[4,64,768]{2,1,0:T(8,128)(2,1)} %get-tuple-element.7, bf16[768,1856,1]{1,0,2:T(8,128)(2,1)} %bitcast.18), kind=kOutput, calls=%fused_computation.13 | convolution fusion | flops 729808896 | bytes 5144576 | tf_op jit(solution)/shard_map/ind,dc->inc/dot_general | solution.py:507
  110.4 1.1 fusion.1
  (4 shorter events, 0.0 us)
Async XLA Ops:
  0.0 5.8 %copy-start = (bf16[768,3,384]{2,0,1:T(8,128)(2,1)S(1)}, bf16[768,3,384]{2,0,1:T(8,128)(2,1)}, u32[]{:S(2)}) copy-start(bf16[768,3,384]{2,0,1:T(8,128)(2,1)} %param.16) | copy-start | bytes 5308420
